TPU v7x, 256 devices: a whole 4x4x8 slice. The times are simulated.
256 devices in a mesh: fsdp: 32 (over x_lo, z, core), seq: 8 (over y, x_hi).
Axes of the slice: x: 4 (x_hi: 2, x_lo: 2; x = x_hi * 2 + x_lo), y: 4, z: 8, core: 2. Of those that a mesh axis runs over, the one named last changes fastest.
Arguments:
- queries: bfloat16 [32, 1024, 3072], P('fsdp', 'seq'), may hold values from -128 to 128
- keys: bfloat16 [32, 1024, 3072], P('fsdp', 'seq'), may hold values from -4 to 4
- values: bfloat16 [32, 1024, 3072], P('fsdp', 'seq'), may hold values from -5 to 5
- query_tangent: bfloat16 [32, 1024, 3072], P('fsdp', 'seq'), may hold values from -5 to 5
- key_tangent: bfloat16 [32, 1024, 3072], P('fsdp', 'seq'), may hold values from -5 to 5
- value_tangent: bfloat16 [32, 1024, 3072], P('fsdp', 'seq'), may hold values from -5 to 5
- out_weight: bfloat16 [3072, 6144], P('seq', 'fsdp'), may hold values from -0.109375 to 0.109375
Outputs:
- mixed: bfloat16 [32, 1024, 6144], P('fsdp', 'seq')
- mixed_tangent: bfloat16 [32, 1024, 6144], P('fsdp', 'seq')
All inputs are finite; a program needn't handle non-finite values.
Results may differ from a plain program's by a relative error of at most 0.017.
Values may be sent and summed in bfloat16 or wider, within the bound.
A program may use at most 128 MiB of HBM per device.

v0:
```python
import math

import jax
import jax.numpy as jnp
from jax import lax
from jax.sharding import PartitionSpec as P

HD = 128


def attend_block(query, query_dot, key_rows, value_rows, key_dot, value_dot):
    scale = 1.0 / math.sqrt(query.shape[2])
    scores = jnp.einsum("qgd,kgd->gqk", query, key_rows, preferred_element_type=jnp.float32) * scale
    scores_dot = (
        jnp.einsum("qgd,kgd->gqk", query_dot, key_rows, preferred_element_type=jnp.float32)
        + jnp.einsum("qgd,kgd->gqk", query, key_dot, preferred_element_type=jnp.float32)
    ) * scale
    peak = jnp.max(scores, axis=-1, keepdims=True)
    expo = jnp.exp(scores - peak)
    probs = expo / jnp.sum(expo, axis=-1, keepdims=True)
    probs_dot = probs * (scores_dot - jnp.sum(probs * scores_dot, axis=-1, keepdims=True))
    probs_low = probs.astype(jnp.bfloat16)
    probs_dot_low = probs_dot.astype(jnp.bfloat16)
    out = jnp.einsum(
        "gqk,kgd->qgd", probs_low, value_rows, preferred_element_type=jnp.float32
    ).astype(jnp.bfloat16)
    out_dot = (
        jnp.einsum("gqk,kgd->qgd", probs_dot_low, value_rows, preferred_element_type=jnp.float32)
        + jnp.einsum("gqk,kgd->qgd", probs_low, value_dot, preferred_element_type=jnp.float32)
    ).astype(jnp.bfloat16)
    return (out, out_dot)


def body(queries, keys, values, query_tangent, key_tangent, value_tangent, out_weight):
    head_size = HD
    local = (queries[0], keys[0], values[0], query_tangent[0], key_tangent[0], value_tangent[0])
    grouped = (
        lax.all_to_all(local[0], "seq", split_axis=1, concat_axis=0, tiled=True),
        lax.all_to_all(local[1], "seq", split_axis=1, concat_axis=0, tiled=True),
        lax.all_to_all(local[2], "seq", split_axis=1, concat_axis=0, tiled=True),
        lax.all_to_all(local[3], "seq", split_axis=1, concat_axis=0, tiled=True),
        lax.all_to_all(local[4], "seq", split_axis=1, concat_axis=0, tiled=True),
        lax.all_to_all(local[5], "seq", split_axis=1, concat_axis=0, tiled=True),
    )
    length = grouped[0].shape[0]
    width = grouped[0].shape[1]
    group_heads = width // head_size
    query, key_rows, value_rows, query_dot, key_dot, value_dot = tuple(
        (array.reshape(length, group_heads, head_size) for array in grouped)
    )
    block = min(512, length)
    blocks = length // block
    query_blocks = query.reshape(blocks, block, group_heads, head_size)
    query_dot_blocks = query_dot.reshape(blocks, block, group_heads, head_size)

    def one_block(pair):
        return attend_block(pair[0], pair[1], key_rows, value_rows, key_dot, value_dot)

    out, out_dot = lax.map(one_block, (query_blocks, query_dot_blocks))
    out = out.reshape(length, width)
    out_dot = out_dot.reshape(length, width)
    rows_weight = lax.all_gather(out_weight, "fsdp", axis=1, tiled=True)
    model_width = rows_weight.shape[1]
    summed = lax.psum_scatter(
        jnp.concatenate(
            [
                jnp.dot(out, rows_weight, preferred_element_type=jnp.float32),
                jnp.dot(out_dot, rows_weight, preferred_element_type=jnp.float32),
            ],
            axis=1,
        ).astype(jnp.bfloat16),
        "seq",
        scatter_dimension=0,
        tiled=True,
    ).astype(jnp.float32)
    mixed = summed[:, :model_width].astype(jnp.bfloat16)
    mixed_tangent = summed[:, model_width:].astype(jnp.bfloat16)
    return (mixed[None], mixed_tangent[None])


def solution(mesh):
    placed = (
        P("fsdp", "seq", None),
        P("fsdp", "seq", None),
        P("fsdp", "seq", None),
        P("fsdp", "seq", None),
        P("fsdp", "seq", None),
        P("fsdp", "seq", None),
        P("seq", "fsdp"),
    )
    return jax.shard_map(
        body,
        mesh=mesh,
        in_specs=placed,
        out_specs=(P("fsdp", "seq", None), P("fsdp", "seq", None)),
        check_vma=False,
    )
```

profile of v0, /device:TPU:1, one launch (start us, length us, event | category | flops | bytes accessed | tf_op | source)
XLA Modules:
  0.0 490.4 jit_solution(6917657484512541056)
XLA Ops:
  7.2 2.4 copy.23
  9.6 7.5 %all-to-all-start = ((bf16[128,8,384]{0,2,1:T(8,128)(2,1)}), bf16[128,8,384]{0,2,1:T(8,128)(2,1)S(1)}, u32[]{:S(2)}, u32[]{:S(2)}) async-start(bf16[128,8,384]{0,2,1:T(8,128)(2,1)} %bitcast.6), calls=%async_computation | async-start | bytes 1572864 | tf_op jit(solution)/shard_map/all_to_all | solution.py:38
  17.1 2.3 copy.25
  19.4 10.9 %all-to-all-done = bf16[128,8,384]{0,2,1:T(8,128)(2,1)S(1)} async-done(((bf16[128,8,384]{0,2,1:T(8,128)(2,1)}), bf16[128,8,384]{0,2,1:T(8,128)(2,1)S(1)}, u32[]{:S(2)}, u32[]{:S(2)}) %all-to-all-start) | async-done | bytes 786464 | tf_op jit(solution)/shard_map/all_to_all | solution.py:38
  30.3 3.8 all-to-all-start.1
  34.1 1.2 copy.27
  35.2 11.4 %all-to-all-done.1 = bf16[128,8,384]{0,2,1:T(8,128)(2,1)S(1)} async-done(((bf16[128,8,384]{0,2,1:T(8,128)(2,1)}), bf16[128,8,384]{0,2,1:T(8,128)(2,1)S(1)}, u32[]{:S(2)}, u32[]{:S(2)}) %all-to-all-start.1) | async-done | bytes 786464 | tf_op jit(solution)/shard_map/all_to_all | solution.py:39
  46.6 3.5 all-to-all-start.2
  50.2 1.2 copy.29
  51.4 10.2 %all-to-all-done.2 = bf16[128,8,384]{0,2,1:T(8,128)(2,1)S(1)} async-done(((bf16[128,8,384]{0,2,1:T(8,128)(2,1)}), bf16[128,8,384]{0,2,1:T(8,128)(2,1)S(1)}, u32[]{:S(2)}, u32[]{:S(2)}) %all-to-all-start.2) | async-done | bytes 786464 | tf_op jit(solution)/shard_map/all_to_all | solution.py:40
  61.6 3.5 all-to-all-start.3
  65.1 2.3 copy.31
  67.4 8.2 %all-to-all-done.3 = bf16[128,8,384]{0,2,1:T(8,128)(2,1)S(1)} async-done(((bf16[128,8,384]{0,2,1:T(8,128)(2,1)}), bf16[128,8,384]{0,2,1:T(8,128)(2,1)S(1)}, u32[]{:S(2)}, u32[]{:S(2)}) %all-to-all-start.3) | async-done | bytes 786464 | tf_op jit(solution)/shard_map/all_to_all | solution.py:41
  75.6 4.2 all-to-all-start.4
  79.9 2.3 copy.33
  82.2 8.2 %all-to-all-done.4 = bf16[128,8,384]{0,2,1:T(8,128)(2,1)} async-done(((bf16[128,8,384]{0,2,1:T(8,128)(2,1)}), bf16[128,8,384]{0,2,1:T(8,128)(2,1)}, u32[]{:S(2)}, u32[]{:S(2)}) %all-to-all-start.4) | async-done | bytes 786464 | tf_op jit(solution)/shard_map/all_to_all | solution.py:42
  90.4 4.2 all-to-all-start.5
  95.5 1.4 copy.24
  96.9 2.0 reshape_reshape.6
  98.9 1.8 copy.35
  102.8 1.2 copy.37
  105.5 1.6 copy.32
  107.5 1.2 copy.39
  108.7 1.6 copy.34
  110.6 1.2 copy.40
  111.8 39.9 %while.12 = (s32[]{:T(128)}, bf16[2,512,3,128]{3,1,2,0:T(8,128)(2,1)}, bf16[2,512,3,128]{3,1,2,0:T(8,128)(2,1)}, bf16[2,512,3,128]{3,1,2,0:T(8,128)(2,1)}, bf16[...) while((s32[]{:T(128)}, ...), condition=%wide.region_4.5_spmd, body=%wide.region_0.4_spmd.sunk | while | flops 2441674240 | bytes 115261824 | solution.py:59
  111.8 3.6 fusion.100
  115.4 4.6 fusion.98
  120.0 5.8 %multiply_reduce_fusion.3 = (f32[3,512]{1,0:T(4,128)S(1)}, f32[3,512,1024]{2,1,0:T(8,128)S(1)}) fusion(f32[3,512,1024]{2,1,0:T(8,128)} %get-tuple-element.153, f32[3,512]{1,0:T(4,128)S(1)} %get-tuple-element.154, f32[3,512,1024]{2,1,0:T(8,128)} %fusion.100, bf16[1024,3,128]{2,0,1:T(8,128)(2,1)S(1)} %copy-done.4, ...), kind=kOutput, calls=%fused_computation.2.clone.1 | convolution fusion | flops 410515968 | bytes 20068356 | tf_op jit(solution)/shard_map/while/body/eval_jaxpr/qgd,kgd->gqk/dot_general | solution.py:16
  125.8 1.1 copy-done.11
  126.9 1.6 fusion.101
  128.5 1.2 fusion.102
  129.7 1.1 fusion.99
  131.8 3.6 fusion.100
  135.3 4.6 fusion.98
  140.0 5.8 %multiply_reduce_fusion.3 = (f32[3,512]{1,0:T(4,128)S(1)}, f32[3,512,1024]{2,1,0:T(8,128)S(1)}) fusion(f32[3,512,1024]{2,1,0:T(8,128)} %get-tuple-element.153, f32[3,512]{1,0:T(4,128)S(1)} %get-tuple-element.154, f32[3,512,1024]{2,1,0:T(8,128)} %fusion.100, bf16[1024,3,128]{2,0,1:T(8,128)(2,1)S(1)} %copy-done.4, ...), kind=kOutput, calls=%fused_computation.2.clone.1 | convolution fusion | flops 410515968 | bytes 20068356 | tf_op jit(solution)/shard_map/while/body/eval_jaxpr/qgd,kgd->gqk/dot_general | solution.py:16
  145.8 1.1 copy-done.11
  146.9 1.6 fusion.101
  148.5 1.2 fusion.102
  149.7 1.1 fusion.99
  151.7 2.3 copy.42
  154.2 2.3 copy.41
  156.6 17.6 %all-gather.2.cloned.1.call-done = bf16[384,6144]{0,1:T(8,128)(2,1)} async-done(((bf16[384,192]{0,1:T(8,128)(2,1)}), bf16[384,6144]{0,1:T(8,128)(2,1)}) %all-gather.2.cloned.1.call-update) | async-done | bytes 4718608 | tf_op jit(solution)/shard_map/all_gather | solution.py:62
  174.2 12.2 %convolution_convert_fusion.1 = bf16[1024,6144]{1,0:T(8,128)(2,1)} fusion(bf16[1024,384]{0,1:T(8,128)(2,1)S(1)} %bitcast.113, bf16[384,6144]{0,1:T(8,128)(2,1)} %all-gather.2.cloned.1.call-done), kind=kOutput, calls=%fused_computation.40 | convolution fusion | flops 4838129664 | bytes 18087936 | tf_op jit(solution)/shard_map/dot_general | solution.py:67
  186.4 9.6 %convolution_convert_fusion = bf16[1024,6144]{1,0:T(8,128)(2,1)} fusion(bf16[1024,384]{0,1:T(8,128)(2,1)S(1)} %bitcast.112, bf16[384,6144]{0,1:T(8,128)(2,1)S(1)} %copy-done.10), kind=kOutput, calls=%fused_computation.39 | convolution fusion | flops 4838129664 | bytes 18087936 | tf_op jit(solution)/shard_map/dot_general | solution.py:68
  196.1 17.5 %pad_maximum_fusion = bf16[1024,12288]{1,0:T(8,128)(2,1)} fusion(bf16[1024,6144]{1,0:T(8,128)(2,1)} %convolution_convert_fusion, bf16[1024,6144]{1,0:T(8,128)(2,1)} %convolution_convert_fusion.1), kind=kLoop, calls=%fused_computation.38 | loop fusion | flops 50331648 | bytes 50331648 | tf_op jit(solution)/shard_map/concatenate | solution.py:65
  213.6 266.1 %reduce-scatter.2.cloned.1.call-done = bf16[128,12288]{1,0:T(8,128)(2,1)} async-done(((bf16[1024,12288]{1,0:T(8,128)(2,1)}), bf16[128,12288]{1,0:T(8,128)(2,1)}) %reduce-scatter.2.cloned.1.call-update) | async-done | bytes 3145744 | tf_op jit(solution)/shard_map/reduce_scatter | solution.py:64
  479.7 3.9 slice_bitcast_fusion
  (59 shorter events, 7.1 us)
Async XLA Ops:
  7.2 26.9 %copy-start = (bf16[1,128,3072]{2,1,0:T(8,128)(2,1)S(1)}, bf16[1,128,3072]{2,1,0:T(8,128)(2,1)}, u32[]{:S(2)}) copy-start(bf16[1,128,3072]{2,1,0:T(8,128)(2,1)} %param.11) | copy-start | bytes 2359300
  7.2 43.0 %copy-start.1 = (bf16[1,128,3072]{2,1,0:T(8,128)(2,1)S(1)}, bf16[1,128,3072]{2,1,0:T(8,128)(2,1)}, u32[]{:S(2)}) copy-start(bf16[1,128,3072]{2,1,0:T(8,128)(2,1)} %param.12) | copy-start | bytes 2359300
  9.6 20.7 %all-to-all-start = ((bf16[128,8,384]{0,2,1:T(8,128)(2,1)}), bf16[128,8,384]{0,2,1:T(8,128)(2,1)S(1)}, u32[]{:S(2)}, u32[]{:S(2)}) async-start(bf16[128,8,384]{0,2,1:T(8,128)(2,1)} %bitcast.6), calls=%async_computation | async-start | bytes 1572864 | tf_op jit(solution)/shard_map/all_to_all | solution.py:38
  30.3 16.4 %all-to-all-start.1 = ((bf16[128,8,384]{0,2,1:T(8,128)(2,1)}), bf16[128,8,384]{0,2,1:T(8,128)(2,1)S(1)}, u32[]{:S(2)}, u32[]{:S(2)}) async-start(bf16[128,8,384]{0,2,1:T(8,128)(2,1)} %bitcast.8), calls=%async_computation.1 | async-start | bytes 1572864 | tf_op jit(solution)/shard_map/all_to_all | solution.py:39
  46.6 14.9 %all-to-all-start.2 = ((bf16[128,8,384]{0,2,1:T(8,128)(2,1)}), bf16[128,8,384]{0,2,1:T(8,128)(2,1)S(1)}, u32[]{:S(2)}, u32[]{:S(2)}) async-start(bf16[128,8,384]{0,2,1:T(8,128)(2,1)} %bitcast.10), calls=%async_computation.2 | async-start | bytes 1572864 | tf_op jit(solution)/shard_map/all_to_all | solution.py:40
  61.6 14.1 %all-to-all-start.3 = ((bf16[128,8,384]{0,2,1:T(8,128)(2,1)}), bf16[128,8,384]{0,2,1:T(8,128)(2,1)S(1)}, u32[]{:S(2)}, u32[]{:S(2)}) async-start(bf16[128,8,384]{0,2,1:T(8,128)(2,1)} %bitcast.108), calls=%async_computation.3 | async-start | bytes 1572864 | tf_op jit(solution)/shard_map/all_to_all | solution.py:41
  75.6 14.8 %all-to-all-start.4 = ((bf16[128,8,384]{0,2,1:T(8,128)(2,1)}), bf16[128,8,384]{0,2,1:T(8,128)(2,1)}, u32[]{:S(2)}, u32[]{:S(2)}) async-start(bf16[128,8,384]{0,2,1:T(8,128)(2,1)} %bitcast.109), calls=%async_computation.4 | async-start | bytes 1572864 | tf_op jit(solution)/shard_map/all_to_all | solution.py:42
  90.4 18.2 %all-to-all-start.5 = ((bf16[128,8,384]{0,2,1:T(8,128)(2,1)}), bf16[128,8,384]{0,2,1:T(8,128)(2,1)}, u32[]{:S(2)}, u32[]{:S(2)}) async-start(bf16[128,8,384]{0,2,1:T(8,128)(2,1)} %bitcast.107), calls=%async_computation.5 | async-start | bytes 1572864 | tf_op jit(solution)/shard_map/all_to_all | solution.py:43
  94.7 79.5 %all-gather.2.cloned.1.call-start = ((), (), s32[]{:S(2)}) async-start(), calls=%async_computation.7 | async-start | bytes 4866048 | tf_op jit(solution)/shard_map/all_gather | solution.py:62
  95.4 384.3 %reduce-scatter.2.cloned.1.call-start = ((), (), s32[]{:S(2)}) async-start(), calls=%async_computation.8 | async-start | bytes 28311552 | tf_op jit(solution)/shard_map/reduce_scatter | solution.py:64
  111.8 3.6 copy-start.2
  111.8 8.2 %copy-start.4 = (bf16[1024,3,128]{2,0,1:T(8,128)(2,1)S(1)}, bf16[1024,3,128]{2,0,1:T(8,128)(2,1)}, u32[]{:S(2)}) copy-start(bf16[1024,3,128]{2,0,1:T(8,128)(2,1)} %get-tuple-element.184) | copy-start | bytes 2359300 | tf_op jit(solution)/shard_map/while
  120.0 5.8 %copy-start.3 = (bf16[1024,3,128]{2,0,1:T(8,128)(2,1)S(1)}, bf16[1024,3,128]{2,0,1:T(8,128)(2,1)}, u32[]{:S(2)}) copy-start(bf16[1024,3,128]{2,0,1:T(8,128)(2,1)} %get-tuple-element.182) | copy-start | bytes 2359300 | tf_op jit(solution)/shard_map/while
  120.0 6.9 %copy-start.11 = (f32[3,512,1024]{2,1,0:T(8,128)S(1)}, f32[3,512,1024]{2,1,0:T(8,128)}, u32[]{:S(2)}) copy-start(f32[3,512,1024]{2,1,0:T(8,128)} %get-tuple-element.153) | copy-start | bytes 18874372 | tf_op jit(solution)/shard_map/while
  126.9 1.6 copy-start.5
  126.9 1.6 copy-start.6
  128.5 1.2 copy-start.8
  129.7 1.2 copy-start.7
  130.9 0.9 copy-start.9
  131.7 3.6 copy-start.2
  131.8 8.2 %copy-start.4 = (bf16[1024,3,128]{2,0,1:T(8,128)(2,1)S(1)}, bf16[1024,3,128]{2,0,1:T(8,128)(2,1)}, u32[]{:S(2)}) copy-start(bf16[1024,3,128]{2,0,1:T(8,128)(2,1)} %get-tuple-element.184) | copy-start | bytes 2359300 | tf_op jit(solution)/shard_map/while
  140.0 5.8 %copy-start.3 = (bf16[1024,3,128]{2,0,1:T(8,128)(2,1)S(1)}, bf16[1024,3,128]{2,0,1:T(8,128)(2,1)}, u32[]{:S(2)}) copy-start(bf16[1024,3,128]{2,0,1:T(8,128)(2,1)} %get-tuple-element.182) | copy-start | bytes 2359300 | tf_op jit(solution)/shard_map/while
  140.0 6.9 %copy-start.11 = (f32[3,512,1024]{2,1,0:T(8,128)S(1)}, f32[3,512,1024]{2,1,0:T(8,128)}, u32[]{:S(2)}) copy-start(f32[3,512,1024]{2,1,0:T(8,128)} %get-tuple-element.153) | copy-start | bytes 18874372 | tf_op jit(solution)/shard_map/while
  146.9 1.6 copy-start.5
  146.9 1.6 copy-start.6
  148.4 1.2 copy-start.8
  149.7 1.2 copy-start.7
  150.8 0.9 copy-start.9
  174.2 12.2 %copy-start.10 = (bf16[384,6144]{0,1:T(8,128)(2,1)S(1)}, bf16[384,6144]{0,1:T(8,128)(2,1)}, u32[]{:S(2)}) copy-start(bf16[384,6144]{0,1:T(8,128)(2,1)} %all-gather.2.cloned.1.call-done) | copy-start | bytes 14155780
Sparse Core Ops, SparseCore 0:
  97.4 76.8 all-gather.1
  213.7 265.9 reduce-scatter.1
where the time goes:
time: 491 us; the launch traced here: 490 us
  waiting for transfers between devices  333 us (68%)
  matrix products  57.6 us (12%)
  local copies, waits for them, and re-layouts  40.6 us (8%)
  starting transfers between devices  26.9 us (5%)
  other arithmetic  17.5 us (4%)
  between operations  14.2 us (3%)
    reduce_scatter x1, waiting for transfers between devices, body(): lax.psum_scatter(jnp.concatenate([jnp.dot(out, rows_weight, preferred_ele...  266 us
    all_gather x1, waiting for transfers between devices, body(): rows_weight = lax.all_gather(out_weight, 'fsdp', axis=1, tiled=True)  17.6 us
    concatenate x1, other arithmetic, body(): jnp.concatenate([jnp.dot(out, rows_weight, preferred_element_type=jnp.flo...  17.5 us
    dot_general x1, matrix products, body(): jnp.dot(out, rows_weight, preferred_element_type=jnp.float32)  12.2 us
    unnamed x14, local copies, waits for them, and re-layouts  11.9 us
    dot_general x2, matrix products, attend_block(): jnp.einsum('qgd,kgd->gqk', query, key_dot, preferred_element_type=jnp.flo...  11.5 us
    all_to_all x1, waiting for transfers between devices, body(): lax.all_to_all(local[1], 'seq', split_axis=1, concat_axis=0, tiled=True)  11.4 us
    while x8, local copies, waits for them, and re-layouts, body(): out, out_dot = lax.map(one_block, (query_blocks, query_dot_blocks))  11 us
  transfers between devices with their start and end apart: 8, of which 7 were waited for; matrix products, arithmetic and copies ran while one was open for 13% of the time, Pallas kernels for 0%

commit v1 on v0

v1 whole, which is shorter than its diff:
```python
import math

import jax
import jax.numpy as jnp
from jax import lax
from jax.experimental import pallas as pl
from jax.experimental.pallas import tpu as pltpu
from jax.sharding import PartitionSpec as P

HD = 128
MESH = pl.DeviceIdType.MESH
F32 = jnp.float32
BF16 = jnp.bfloat16
SCALE = 1.0 / math.sqrt(HD)


def kernel(q, k, v, qd, kd, vd, w, mixed, mixed_dot, W, inb, stage, a_p, a_q, acc, ob, wx,
           in_send, in_recv, in_loc, out_send, out_recv, wsend, wrecv, osem):
    f, s = lax.axis_index("fsdp"), lax.axis_index("seq")
    xlo, z, c = f // 16, (f // 2) % 8, f % 2
    y, xhi = s // 2, s % 2
    x = xhi * 2 + xlo
    peer = 1 - c
    z4 = (z + 4) % 8

    def dev(dx=0, dy=0, dz=0, core=None):
        xx, yy, zz = (x + dx) % 4, (y + dy) % 4, (z + dz) % 8
        return ((xx % 2) * 16 + zz * 2 + (c if core is None else core), yy * 2 + xx // 2)

    mate = dev(core=peer)

    barrier = pltpu.get_barrier_semaphore()

    def greet(device):
        pl.semaphore_signal(barrier, inc=1, device_id=device, device_id_type=MESH)

    def greet_seq(j, carry):
        greet((f, (s + j) % 8))
        return carry

    def greet_z(j, carry):
        greet(dev(dz=j))
        return carry

    lax.fori_loop(1, 8, greet_seq, 0)
    lax.fori_loop(1, 8, greet_z, 0)
    greet(mate)
    greet(dev(dx=1))
    greet(dev(dx=3))
    pl.semaphore_wait(barrier, 17)

    count = [0]

    def push(part, device, sem=None):
        if sem is None:
            sem = count[0]
            count[0] += 1
        pltpu.make_async_remote_copy(
            src_ref=part, dst_ref=part, send_sem=wsend.at[sem], recv_sem=wrecv.at[sem],
            device_id=device, device_id_type=MESH,
        ).start()
        return sem

    sent = []

    def landed(part, sem):
        pltpu.make_async_copy(part, part, wrecv.at[sem]).wait()
        sent.append((part, sem))

    def landed_later(part, sem):
        sent.append((part, sem))

    arrays = (qd, q, k, kd, v, vd)

    def send_in(h):
        def to(j, carry):
            t = (s + j) % 8
            for i, ref in enumerate(arrays):
                pltpu.make_async_remote_copy(
                    src_ref=ref.at[0, :, pl.ds(pl.multiple_of(t * 384 + h * HD, HD), HD)],
                    dst_ref=inb.at[h, s, :, pl.ds(i * HD, HD)],
                    send_sem=in_send.at[h], recv_sem=in_recv.at[h],
                    device_id=(f, t), device_id_type=MESH,
                ).start()
            return carry

        lax.fori_loop(1, 8, to, 0)
        for i, ref in enumerate(arrays):
            pltpu.make_async_copy(
                ref.at[0, :, pl.ds(pl.multiple_of(s * 384 + h * HD, HD), HD)],
                inb.at[h, s, :, pl.ds(i * HD, HD)],
                in_loc.at[h],
            ).start()

    def wait_in(h):
        pltpu.make_async_copy(inb.at[h, pl.ds(0, 7)], inb.at[h, pl.ds(0, 7)], in_recv.at[h]).wait()
        pltpu.make_async_copy(inb.at[h, s], inb.at[h, s], in_loc.at[h]).wait()

    def attend(h):
        def block(b, carry):
            qq = inb[h, pl.ds(2 * b, 2), :, 0:256].reshape(256, 256)
            kk = inb[h, :, :, 256:512].reshape(1024, 256)
            vv = inb[h, :, :, 512:768].reshape(1024, 256)
            nt = (((1,), (1,)), ((), ()))
            scores = lax.dot_general(qq[:, 128:], kk[:, :128], nt, preferred_element_type=F32)
            scores_dot = lax.dot_general(qq, kk, nt, preferred_element_type=F32)
            peak = jnp.max(scores, axis=1, keepdims=True)
            expo = jnp.exp((scores - peak) * SCALE)
            inv = 1.0 / jnp.sum(expo, axis=1, keepdims=True)
            mean = jnp.sum(expo * scores_dot, axis=1, keepdims=True) * inv
            probs = expo * inv
            probs_dot = (expo * (inv * SCALE)) * (scores_dot - mean)
            both = jnp.dot(probs.astype(BF16), vv, preferred_element_type=F32)
            out_dot = both[:, 128:] + jnp.dot(probs_dot.astype(BF16), vv[:, :128], preferred_element_type=F32)
            stage[h, pl.ds(2 * b, 2), 0] = both[:, :128].astype(BF16).reshape(2, 128, HD)
            stage[h, pl.ds(2 * b, 2), 1] = out_dot.astype(BF16).reshape(2, 128, HD)
            return carry

        lax.fori_loop(0, 4, block, 0)

    def out_slot(h, t):
        if h == 2:
            return a_q.at[:, :, pl.ds(pl.multiple_of(t * HD, HD), HD)]
        return a_p.at[:, :, pl.ds(pl.multiple_of(t * 256 + h * HD, HD), HD)]

    def send_out(h):
        def to(j, carry):
            t = (s + j) % 8
            pltpu.make_async_remote_copy(
                src_ref=stage.at[h, t], dst_ref=out_slot(h, s),
                send_sem=out_send.at[h], recv_sem=out_recv.at[h],
                device_id=(f, t), device_id_type=MESH,
            ).start()
            return carry

        lax.fori_loop(1, 8, to, 0)
        out_slot(h, s)[...] = stage[h, s]

    def wait_out(h):
        pltpu.make_async_copy(stage.at[h, pl.ds(0, 7)], stage.at[h, pl.ds(0, 7)], out_recv.at[h]).wait()

    def lanes(xl):
        return pl.ds(pl.multiple_of(xl * 384, HD), 384)

    xm, xp = (x + 3) % 4, (x + 1) % 4
    ym, yp = (y + 3) % 4, (y + 1) % 4

    def prepare_send():
        for h in range(3):
            pltpu.make_async_remote_copy(
                src_ref=w.at[pl.ds(pl.multiple_of(h * 128 + peer * 64, 64), 64)], dst_ref=wx.at[h],
                send_sem=osem.at[1], recv_sem=osem.at[2],
                device_id=mate, device_id_type=MESH,
            ).start()

    def prepare():
        pltpu.make_async_copy(wx, wx, osem.at[2]).wait()
        row = lax.broadcasted_iota(jnp.int32, (192, 384), 0)
        lane = lax.broadcasted_iota(jnp.int32, (192, 384), 1)
        put_own = (lane == row + 192 * c).astype(BF16)
        put_other = (lane == row + 192 * peer).astype(BF16)
        for h in range(3):
            own = w[pl.ds(pl.multiple_of(h * 128 + c * 64, 64), 64), :]
            both = jnp.dot(own, put_own, preferred_element_type=F32)
            both += jnp.dot(wx[h], put_other, preferred_element_type=F32)
            W[z, y, xhi, h, c, :, lanes(xlo)] = both.astype(BF16)

    mine = lambda h: W.at[z, y, xhi, h, c, :, lanes(xlo)]

    q1 = []

    def q1_send():
        first = count[0]
        count[0] += 7

        def to(j, carry):
            push(mine(2), dev(dz=j), first + j - 1)
            return carry

        lax.fori_loop(1, 8, to, 0)
        q1.append(first)
        q1.append(push(mine(0), dev(dz=4)))
        q1.append(push(mine(1), dev(dz=4)))

    def q1_wait():
        def of(j, carry):
            part = W.at[(z + 8 - j) % 8, y, xhi, 2, c, :, lanes(xlo)]
            pltpu.make_async_copy(part, part, wrecv.at[q1[0] + j - 1]).wait()
            return carry

        lax.fori_loop(1, 8, of, 0)
        landed(W.at[z4, y, xhi, 0, c, :, lanes(xlo)], q1[1])
        landed(W.at[z4, y, xhi, 1, c, :, lanes(xlo)], q1[2])

    p1 = {}

    def p1_first():
        for j in (1, 3, 2):
            p1["a", j] = push(mine(0), dev(dx=j))
            p1["b", j] = push(mine(1), dev(dy=j))

    def p1_second():
        for j in (1, 3, 2):
            from_x, from_y = (x + 4 - j) % 4, (y + 4 - j) % 4
            landed(W.at[z, y, from_x // 2, 0, c, :, lanes(from_x % 2)], p1["a", j])
            landed(W.at[z, from_y, xhi, 1, c, :, lanes(xlo)], p1["b", j])
        for j in (1, 3, 2):
            p1["A", j] = push(W.at[z, y, :, 0, c], dev(dy=j))
            p1["B", j] = push(W.at[z, :, xhi, 1, c, :, lanes(xlo)], dev(dx=j))

    def p1_wait(kind):
        for j in (1, 3, 2):
            from_x, from_y = (x + 4 - j) % 4, (y + 4 - j) % 4
            if kind == "A":
                landed(W.at[z, from_y, :, 0, c], p1["A", j])
            else:
                landed(W.at[z, :, from_x // 2, 1, c, :, lanes(from_x % 2)], p1["B", j])

    ring = {}
    own_peer = {}

    def chunk(slab, h, half, core=None):
        return W.at[slab, pl.ds(2 * half, 2), :, h, c if core is None else core]

    def ring_start(h):
        for half in range(2):
            ring[0, 0, h, half] = push(chunk(z, h, half), dev(dz=1))
            ring[1, 0, h, half] = push(chunk(z, h, half), dev(dz=7))
        own_peer[h] = push(W.at[z, :, :, h, c], mate)

    def slab_of(way, step):
        return (z + 7 - step) % 8 if way == 0 else (z + 1 + step) % 8

    ring_peer = {}

    def ring_turn(step, h, half):
        for way in range(2):
            part = chunk(slab_of(way, step), h, half)
            landed(part, ring[way, step, h, half])
            if step < 2:
                ring[way, step + 1, h, half] = push(part, dev(dz=1 if way == 0 else 7))
            ring_peer[way, step, h, half] = push(part, mate)

    def ring_peer_wait(step):
        for way in range(2):
            for h in range(2):
                for half in range(2):
                    landed(chunk(slab_of(way, step), h, half, peer), ring_peer[way, step, h, half])

    q2 = {}
    group_slabs = {"a": 0, "b": 4}
    group_extra = {"a": 0, "b": 1}

    def parts(group, at, core, half=None):
        first, size, rows = group_slabs[group], 4, slice(None)
        if half is not None:
            first, size, rows = first + 2 * half, 2, pl.ds(32 * half, 32)
        yy, hh, ll = at
        return (W.at[pl.ds(first, size), yy, hh, 2, core, :, ll],
                W.at[z4, yy, hh, group_extra[group], core, rows, ll])

    whole = slice(None)

    def q2_push(key, group, at, device, half=None):
        q2[key] = [push(part, device) for part in parts(group, at, c, half)]

    def q2_landed(key, group, at, half=None, core=None):
        for part, sem in zip(parts(group, at, c if core is None else core, half), q2[key]):
            landed(part, sem)

    def at_x(xx):
        return (y, xx // 2, lanes(xx % 2))

    def at_y(yy):
        return (yy, xhi, lanes(xlo))

    def row_y(yy):
        return (yy, whole, whole)

    def column_x(xx):
        return (whole, xx // 2, lanes(xx % 2))

    plan = {"a": (at_x, x, xm, xp, "x", row_y, y, ym, yp, "y"),
            "b": (at_y, y, ym, yp, "y", column_x, x, xm, xp, "x")}

    def step_to(axis, up):
        return dev(dx=1 if up else 3) if axis == "x" else dev(dy=1 if up else 3)

    def q2_1():
        for g in "ab":
            one, me, lo, hi, axis = plan[g][:5]
            q2_push((g, 1, "up"), g, one(me), step_to(axis, True))
            q2_push((g, 1, "down"), g, one(me), step_to(axis, False))

    def q2_2():
        for g in "ab":
            one, me, lo, hi, axis = plan[g][:5]
            q2_landed((g, 1, "up"), g, one(lo))
            q2_push((g, 2, "up"), g, one(lo), step_to(axis, True), 0)
            q2_landed((g, 1, "down"), g, one(hi))
            q2_push((g, 2, "down"), g, one(hi), step_to(axis, False), 1)

    def q2_3():
        for g in "ab":
            one, me, lo, hi, axis, many, me2, lo2, hi2, axis2 = plan[g]
            q2_landed((g, 2, "up"), g, one((me + 2) % 4), 0)
            q2_landed((g, 2, "down"), g, one((me + 2) % 4), 1)
            q2_push((g, 3, "up"), g, many(me2), step_to(axis2, True))
            q2_push((g, 3, "down"), g, many(me2), step_to(axis2, False))
            q2_push((g, "peer", 0), g, many(me2), mate)

    def q2_4():
        for g in "ab":
            many, me2, lo2, hi2, axis2 = plan[g][5:]
            q2_landed((g, 3, "up"), g, many(lo2))
            q2_push((g, 4, "up"), g, many(lo2), step_to(axis2, True), 0)
            q2_landed((g, 3, "down"), g, many(hi2))
            q2_push((g, 4, "down"), g, many(hi2), step_to(axis2, False), 1)
            q2_push((g, "peer", 3), g, many(lo2), mate)
            q2_push((g, "peer", 1), g, many(hi2), mate)

    def q2_5():
        for g in "ab":
            many, me2 = plan[g][5:7]
            q2_landed((g, 4, "up"), g, many((me2 + 2) % 4), 0)
            q2_landed((g, 4, "down"), g, many((me2 + 2) % 4), 1)
            q2_push((g, "peer", 2), g, many((me2 + 2) % 4), mate)

    def q2_peer_wait():
        for g in "ab":
            many, me2 = plan[g][5:7]
            for j in range(4):
                q2_landed((g, "peer", j), g, many((me2 + j) % 4), core=peer)

    def project(n):
        wide = W[n, :, :, 0:2].reshape(2048, 768)
        acc[n] = jnp.dot(a_p[...].reshape(256, 2048), wide, preferred_element_type=F32)

    def finish(n, carry):
        wide = W[n, :, :, 2].reshape(1024, 768)
        total = acc[n] + jnp.dot(a_q[...].reshape(256, 1024), wide, preferred_element_type=F32)
        ob[n] = total.astype(BF16).reshape(2, 128, 768)
        for i, ref in enumerate((mixed, mixed_dot)):
            for xl in range(2):
                pltpu.make_async_copy(
                    ob.at[n, i, :, pl.ds(xl * 384, 384)],
                    ref.at[0, :, pl.ds(pl.multiple_of(xl * 3072 + n * 384, HD), 384)],
                    osem.at[0],
                ).start()
        return carry

    def project_pair(step):
        def one(way, carry):
            project((z + 7 - step + way * (2 + 2 * step)) % 8)
            return carry

        lax.fori_loop(0, 2, one, 0)

    prepare_send()
    prepare()
    p1_first()
    q1_send()
    send_in(0)
    p1_second()
    send_in(1)
    p1_wait("A")
    ring_start(0)
    p1_wait("B")
    ring_start(1)
    send_in(2)
    wait_in(0)
    attend(0)
    send_out(0)
    q1_wait()
    wait_in(1)
    q2_1()
    attend(1)
    send_out(1)
    for h in range(2):
        for half in range(2):
            ring_turn(0, h, half)
    q2_2()
    wait_in(2)
    attend(2)
    send_out(2)
    q2_3()
    wait_out(0)
    wait_out(1)
    for h in range(2):
        landed(W.at[z, :, :, h, peer], own_peer[h])
    project(z)
    ring_peer_wait(0)
    for h in range(2):
        for half in range(2):
            ring_turn(1, h, half)
    project_pair(0)
    q2_4()
    ring_peer_wait(1)
    project_pair(1)
    wait_out(2)
    q2_5()
    for h in range(2):
        for half in range(2):
            ring_turn(2, h, half)
    q2_peer_wait()
    project(z4)
    ring_peer_wait(2)
    project_pair(2)
    lax.fori_loop(0, 8, finish, 0)

    pltpu.make_async_copy(ob, ob, osem.at[0]).wait()
    pltpu.make_async_copy(wx, wx, osem.at[1]).wait()
    for h in range(3):
        pltpu.make_async_copy(inb.at[h, pl.ds(0, 7)], inb.at[h, pl.ds(0, 7)], in_send.at[h]).wait()
        pltpu.make_async_copy(stage.at[h, pl.ds(0, 7)], stage.at[h, pl.ds(0, 7)], out_send.at[h]).wait()

    def left(j, carry):
        pltpu.make_async_copy(mine(2), mine(2), wsend.at[q1[0] + j]).wait()
        return carry

    lax.fori_loop(0, 7, left, 0)
    for part, sem in sent:
        pltpu.make_async_copy(part, part, wsend.at[sem]).wait()
    assert count[0] <= wsend.shape[0] and len(sent) == count[0] - 7


def body(queries, keys, values, query_tangent, key_tangent, value_tangent, out_weight):
    any_space = pl.BlockSpec(memory_space=pl.ANY)
    shape = jax.ShapeDtypeStruct((1, 128, 6144), BF16)
    return pl.pallas_call(
        kernel,
        name="attend_project",
        out_shape=(shape, shape),
        in_specs=[any_space] * 6 + [pl.BlockSpec(memory_space=pltpu.VMEM)],
        out_specs=(any_space, any_space),
        scratch_shapes=[
            pltpu.VMEM((8, 4, 2, 3, 2, 64, 768), BF16),
            pltpu.VMEM((3, 8, 128, 768), BF16),
            pltpu.VMEM((3, 8, 2, 128, 128), BF16),
            pltpu.VMEM((2, 128, 2048), BF16),
            pltpu.VMEM((2, 128, 1024), BF16),
            pltpu.VMEM((8, 256, 768), F32),
            pltpu.VMEM((8, 2, 128, 768), BF16),
            pltpu.VMEM((3, 64, 192), BF16),
            pltpu.SemaphoreType.DMA((3,)),
            pltpu.SemaphoreType.DMA((3,)),
            pltpu.SemaphoreType.DMA((3,)),
            pltpu.SemaphoreType.DMA((3,)),
            pltpu.SemaphoreType.DMA((3,)),
            pltpu.SemaphoreType.DMA((160,)),
            pltpu.SemaphoreType.DMA((160,)),
            pltpu.SemaphoreType.DMA((3,)),
        ],
        compiler_params=pltpu.CompilerParams(
            collective_id=0, has_side_effects=True, vmem_limit_bytes=62 * 2**20
        ),
        cost_estimate=pl.CostEstimate(
            flops=17 * 10**9, bytes_accessed=8 * 2**20, transcendentals=3 * 2**20
        ),
    )(queries, keys, values, query_tangent, key_tangent, value_tangent, out_weight)


def solution(mesh):
    placed = (P("fsdp", "seq", None),) * 6 + (P("seq", "fsdp"),)
    return jax.shard_map(
        body,
        mesh=mesh,
        in_specs=placed,
        out_specs=(P("fsdp", "seq", None), P("fsdp", "seq", None)),
        check_vma=False,
    )
```

time: 491 us -> 166 us (0.34)
  waiting for transfers between devices: 333 us -> 0 us
  Pallas kernels: 0 us -> 160 us
  matrix products: 57.6 us -> 0 us
  local copies, waits for them, and re-layouts: 40.6 us -> 5.68 us
  starting transfers between devices: 26.9 us -> 0 us
  other arithmetic: 17.5 us -> 0 us
  between operations: 14.2 us -> 0.65 us
    reduce_scatter x1 -> x0, waiting for transfers between devices: 266 us -> none  [body(): lax.psum_scatter(jnp.concatenate([jnp.dot(out, rows_weight, preferred_ele...]
    pallas_call x0 -> x1, Pallas kernels: none -> 160 us  [body(): pl.pallas_call(kernel, name='attend_project', out_shape=(shape, shape), i...]
    all_to_all x6 -> x0, waiting for transfers between devices: 49 us -> none  [the longest x1 11.4 us: body(): lax.all_to_all(local[1], 'seq', split_axis=1, concat_axis=0, tiled=True)]
    dot_general x12 -> x0, matrix products: 48.3 us -> none  [the longest x1 12.2 us: body(): jnp.dot(out, rows_weight, preferred_element_type=jnp.float32)]
    all_to_all x6 -> x0, starting transfers between devices: 26.8 us -> none  [the longest x1 7.48 us: body(): lax.all_to_all(local[0], 'seq', split_axis=1, concat_axis=0, tiled=True)]
    all_gather x1 -> x0, waiting for transfers between devices: 17.6 us -> none  [body(): rows_weight = lax.all_gather(out_weight, 'fsdp', axis=1, tiled=True)]
    concatenate x1 -> x0, other arithmetic: 17.5 us -> none  [body(): jnp.concatenate([jnp.dot(out, rows_weight, preferred_element_type=jnp.flo...]
    while x44 -> x0, local copies, waits for them, and re-layouts: 15 us -> none  [the longest x8 11 us: body(): out, out_dot = lax.map(one_block, (query_blocks, query_dot_blocks))]
  transfers between devices with their start and end apart: 8 -> 0, of which waited for: 7 -> 0; matrix products, arithmetic and copies ran while one was open for 13% -> 0% of each run, Pallas kernels for 0% -> 0%
where the time goes in v1:
time: 166 us
  Pallas kernels  160 us (96%)
  local copies, waits for them, and re-layouts  5.68 us (3%)
    pallas_call x1, Pallas kernels, body(): pl.pallas_call(kernel, name='attend_project', out_shape=(shape, shape), i...  160 us
    unnamed x5, local copies, waits for them, and re-layouts  5.68 us

profile of v1, /device:TPU:1, one launch (start us, length us, event | category | flops | bytes accessed | tf_op | source)
XLA Modules:
  0.0 166.0 jit_solution(12783288274393852945)
XLA Ops:
  0.6 1.7 %copy.9.w = bf16[384,192]{1,0:T(8,128)(2,1)} copy(bf16[384,192]{0,1:T(8,128)(2,1)} %param.13) | data formatting | bytes 294912 | tf_op args[6]
  2.4 159.7 %attend_project.1 = (bf16[1,128,6144]{2,1,0:T(8,128)(2,1)}, bf16[1,128,6144]{2,1,0:T(8,128)(2,1)}) custom-call(bf16[1,128,3072]{2,1,0:T(8,128)(2,1)} %q.1, bf16[1,128,3072]{2,1,0:T(8,128)(2,1)} %k.1, bf16[1,128,3072]{2,1,0:T(8,128)(2,1)} %v.1, bf16[1,128,3072]{2,1,0:T(8,128)(2,1)} %qd.1, bf16[1,128,3072]{2,1,0:T(8,128)(2,1)} %kd.1, ...), custom_call_target="tpu_custom_call" | custom-call | flops 16999999488 | bytes 8388608 | tf_op jit(solution)/shard_map/attend_project/pallas_call | solution.py:430
  162.0 0.0 copy-start
  162.0 2.8 %copy.12 = bf16[1,128,6144]{2,1,0:T(8,128)(2,1)} copy(bf16[1,128,6144]{2,1,0:T(8,128)(2,1)} %get-tuple-element.4) | data formatting | bytes 3145728
  164.8 0.0 copy-done
  164.8 1.1 copy.13
Async XLA Ops:
  162.0 2.8 %copy-start = (bf16[1,128,6144]{2,1,0:T(8,128)(2,1)S(1)}, bf16[1,128,6144]{2,1,0:T(8,128)(2,1)}, u32[]{:S(2)}) copy-start(bf16[1,128,6144]{2,1,0:T(8,128)(2,1)} %get-tuple-element.5) | copy-start | bytes 4718596

commit v2 on v0

v2 whole, which is shorter than its diff:
```python
import math

import jax
import jax.numpy as jnp
from jax import lax
from jax.experimental import pallas as pl
from jax.experimental.pallas import tpu as pltpu
from jax.sharding import PartitionSpec as P

HD = 128
MESH = pl.DeviceIdType.MESH
F32 = jnp.float32
BF16 = jnp.bfloat16
SCALE = 1.0 / math.sqrt(HD)
TURNS = (0, 1, 3, 2)


def kernel(q, k, v, qd, kd, vd, w, mixed, mixed_dot, W, inb, stage, A, ob, wx,
           in_send, in_recv, in_loc, out_send, out_recv, fsend, frecv, wsend, wrecv, osem):
    f, s = lax.axis_index("fsdp"), lax.axis_index("seq")
    xlo, z, c = f // 16, (f // 2) % 8, f % 2
    y, xhi = s // 2, s % 2
    x = xhi * 2 + xlo
    peer = 1 - c
    xm, xp = (x + 3) % 4, (x + 1) % 4

    def dev(dx=0, dy=0, dz=0, core=None):
        xx, yy, zz = (x + dx) % 4, (y + dy) % 4, (z + dz) % 8
        return ((xx % 2) * 16 + zz * 2 + (c if core is None else core), yy * 2 + xx // 2)

    mate = dev(core=peer)

    barrier = pltpu.get_barrier_semaphore()

    def greet(device):
        pl.semaphore_signal(barrier, inc=1, device_id=device, device_id_type=MESH)

    def greet_seq(j, carry):
        greet((f, (s + j) % 8))
        return carry

    def greet_x(j, carry):
        greet(dev(dx=1, dy=j))
        greet(dev(dx=3, dy=j))
        return carry

    lax.fori_loop(1, 8, greet_seq, 0)
    lax.fori_loop(0, 4, greet_x, 0)
    greet(dev(dz=1))
    greet(dev(dz=7))
    greet(mate)
    pl.semaphore_wait(barrier, 18)

    count = [0]
    sent = []

    def push(part, device):
        sem = count[0]
        count[0] += 1
        pltpu.make_async_remote_copy(
            src_ref=part, dst_ref=part, send_sem=wsend.at[sem], recv_sem=wrecv.at[sem],
            device_id=device, device_id_type=MESH,
        ).start()
        return sem

    def landed(part, sem):
        pltpu.make_async_copy(part, part, wrecv.at[sem]).wait()
        sent.append((part, sem))

    arrays = (qd, q, k, kd, v, vd)

    def send_in(h):
        def to(j, carry):
            t = (s + j) % 8
            for i, ref in enumerate(arrays):
                pltpu.make_async_remote_copy(
                    src_ref=ref.at[0, :, pl.ds(pl.multiple_of(t * 384 + h * HD, HD), HD)],
                    dst_ref=inb.at[h, s, :, pl.ds(i * HD, HD)],
                    send_sem=in_send.at[h], recv_sem=in_recv.at[h],
                    device_id=(f, t), device_id_type=MESH,
                ).start()
            return carry

        lax.fori_loop(1, 8, to, 0)
        for i, ref in enumerate(arrays):
            pltpu.make_async_copy(
                ref.at[0, :, pl.ds(pl.multiple_of(s * 384 + h * HD, HD), HD)],
                inb.at[h, s, :, pl.ds(i * HD, HD)],
                in_loc.at[h],
            ).start()

    def wait_in(h):
        pltpu.make_async_copy(inb.at[h, pl.ds(0, 7)], inb.at[h, pl.ds(0, 7)], in_recv.at[h]).wait()
        pltpu.make_async_copy(inb.at[h, s], inb.at[h, s], in_loc.at[h]).wait()

    def lane_of(h, hi, yy):
        return pl.ds(pl.multiple_of(((h * 2 + hi) * 4 + yy) * HD, HD), HD)

    def lanes_of(h, hi):
        return pl.ds(pl.multiple_of((h * 2 + hi) * 512, 512), 512)

    def send_out(h, yy):
        mine = lane_of(h, xhi, y)

        @pl.when(yy == y)
        def _():
            A[0:2, :, mine] = stage[h, yy, xhi]

        @pl.when(yy != y)
        def _():
            pltpu.make_async_remote_copy(
                src_ref=stage.at[h, yy, xhi], dst_ref=A.at[pl.ds(0, 2), :, mine],
                send_sem=out_send.at[h, 0], recv_sem=out_recv.at[h, 0],
                device_id=(f, yy * 2 + xhi), device_id_type=MESH,
            ).start()

        for row, sem, xx in ((0, 1, xm), (1, 2, xp)):
            pltpu.make_async_remote_copy(
                src_ref=stage.at[h, yy, 1 - xhi, row], dst_ref=A.at[row + 2, :, mine],
                send_sem=out_send.at[h, sem], recv_sem=out_recv.at[h, sem],
                device_id=((xx % 2) * 16 + z * 2 + c, yy * 2 + xx // 2), device_id_type=MESH,
            ).start()

    def attend(h):
        def block(b, carry):
            yy = (y + 1 + b) % 4
            qq = inb[h, pl.ds(2 * yy, 2), :, 0:256].reshape(256, 256)
            kk = inb[h, :, :, 256:512].reshape(1024, 256)
            vv = inb[h, :, :, 512:768].reshape(1024, 256)
            nt = (((1,), (1,)), ((), ()))
            scores = lax.dot_general(qq[:, 128:], kk[:, :128], nt, preferred_element_type=F32)
            scores_dot = lax.dot_general(qq, kk, nt, preferred_element_type=F32)
            peak = jnp.max(scores, axis=1, keepdims=True)
            expo = jnp.exp((scores - peak) * SCALE)
            inv = 1.0 / jnp.sum(expo, axis=1, keepdims=True)
            mean = jnp.sum(expo * scores_dot, axis=1, keepdims=True) * inv
            probs = expo * inv
            probs_dot = (expo * (inv * SCALE)) * (scores_dot - mean)
            both = jnp.dot(probs.astype(BF16), vv, preferred_element_type=F32)
            out_dot = both[:, 128:] + jnp.dot(probs_dot.astype(BF16), vv[:, :128], preferred_element_type=F32)
            stage[h, yy, :, 0] = both[:, :128].astype(BF16).reshape(2, 128, HD)
            stage[h, yy, :, 1] = out_dot.astype(BF16).reshape(2, 128, HD)
            send_out(h, yy)
            return carry

        lax.fori_loop(0, 4, block, 0)

    def wait_bytes(part, sem):
        pltpu.make_async_copy(part, part, sem).wait()

    def forward(h, i, src_row, dst_row, hi, dx):
        pltpu.make_async_remote_copy(
            src_ref=A.at[src_row, :, lanes_of(h, hi)], dst_ref=A.at[dst_row, :, lanes_of(h, hi)],
            send_sem=fsend.at[h, i], recv_sem=frecv.at[h, i],
            device_id=dev(dx=dx), device_id_type=MESH,
        ).start()

    def relay_out(h):
        wait_bytes(stage.at[h, pl.ds(0, 3), 0], out_recv.at[h, 0])
        forward(h, 0, 0, 2, xhi, 1)
        forward(h, 1, 1, 3, xhi, 3)
        wait_bytes(A.at[2, :, lanes_of(h, xp // 2)], out_recv.at[h, 1])
        forward(h, 2, 2, 0, xp // 2, 3)
        wait_bytes(A.at[3, :, lanes_of(h, xm // 2)], out_recv.at[h, 2])
        forward(h, 3, 3, 1, xm // 2, 1)

    def wait_out(h):
        wait_bytes(A.at[2, :, lanes_of(h, xm // 2)], frecv.at[h, 0])
        wait_bytes(A.at[3, :, lanes_of(h, xp // 2)], frecv.at[h, 1])
        wait_bytes(A.at[0, :, lanes_of(h, 1 - xhi)], frecv.at[h, 2])
        wait_bytes(A.at[1, :, lanes_of(h, 1 - xhi)], frecv.at[h, 3])

    def prepare_send():
        pltpu.make_async_remote_copy(
            src_ref=w.at[:, peer], dst_ref=wx, send_sem=osem.at[1], recv_sem=osem.at[2],
            device_id=mate, device_id_type=MESH,
        ).start()

    def prepare():
        wait_bytes(wx, osem.at[2])
        row = lax.broadcasted_iota(jnp.int32, (192, 384), 0)
        lane = lax.broadcasted_iota(jnp.int32, (192, 384), 1)
        put_own = (lane == row + 192 * c).astype(BF16)
        put_other = (lane == row + 192 * peer).astype(BF16)
        own = w[:, c].reshape(192, 192)
        both = jnp.dot(own, put_own, preferred_element_type=F32)
        both += jnp.dot(wx[...].reshape(192, 192), put_other, preferred_element_type=F32)
        W[z, :, xhi, y, c] = both.astype(BF16).reshape(3, 64, 384)

    def chunk(slab, turn, core=None):
        return W.at[slab, :, :, (y + turn) % 4, c if core is None else core]

    plane = {}
    ring = {}
    mates = {}

    def plane_x():
        plane["x"] = push(W.at[z, :, xhi, y, c], dev(dx=2))

    def plane_y():
        landed(W.at[z, :, 1 - xhi, y, c], plane["x"])
        for turn in (1, 3, 2):
            plane[turn] = push(chunk(z, 0), dev(dy=4 - turn))

    def ring_start(j):
        turn = TURNS[j]
        if turn:
            landed(chunk(z, turn), plane[turn])
        ring[0, 0, j] = push(chunk(z, turn), dev(dz=1))
        ring[1, 0, j] = push(chunk(z, turn), dev(dz=7))
        mates["own", j] = push(chunk(z, turn), mate)

    def slab_of(way, step):
        return (z + 7 - step) % 8 if way == 0 else (z + 1 + step) % 8

    def ways(step, j):
        return (0, 1) if step < 3 else ((0,) if j < 2 else (1,))

    def ring_turn(step, j):
        for way in ways(step, j):
            part = chunk(slab_of(way, step), TURNS[j])
            landed(part, ring[way, step, j])
            if step < 3 and way in ways(step + 1, j):
                ring[way, step + 1, j] = push(part, dev(dz=1 if way == 0 else 7))
            mates[way, step, j] = push(part, mate)

    def slab_wait(way, step):
        for j in range(4):
            if step is None:
                landed(chunk(z, TURNS[j], peer), mates["own", j])
            elif step < 3:
                landed(chunk(slab_of(way, step), TURNS[j], peer), mates[way, step, j])
            else:
                own_way = ways(3, j)[0]
                landed(chunk(slab_of(own_way, 3), TURNS[j], peer), mates[own_way, 3, j])

    def project(n):
        total = jnp.dot(A[...].reshape(512, 3072), W[n].reshape(3072, 384), preferred_element_type=F32)
        ob[n] = total.astype(BF16).reshape(4, 128, 384)
        columns = pl.ds(pl.multiple_of(xlo * 3072 + n * 384, HD), 384)
        for row, ref, dx in ((2, mixed, 3), (3, mixed_dot, 1)):
            pltpu.make_async_remote_copy(
                src_ref=ob.at[n, row], dst_ref=ref.at[0, :, columns],
                send_sem=osem.at[3], recv_sem=osem.at[4],
                device_id=dev(dx=dx), device_id_type=MESH,
            ).start()
        for row, ref in ((0, mixed), (1, mixed_dot)):
            pltpu.make_async_copy(ob.at[n, row], ref.at[0, :, columns], osem.at[0]).start()

    def project_pair(step):
        def one(way, carry):
            project((z + 7 - step + way * (2 + 2 * step)) % 8)
            return carry

        lax.fori_loop(0, 2, one, 0)

    prepare_send()
    prepare()
    plane_x()
    plane_y()
    ring_start(0)
    send_in(0)
    send_in(1)
    send_in(2)
    ring_start(1)
    ring_start(2)
    ring_start(3)
    ring_turn(0, 0)
    ring_turn(0, 1)
    wait_in(0)
    attend(0)
    ring_turn(0, 2)
    ring_turn(0, 3)
    ring_turn(1, 0)
    relay_out(0)
    ring_turn(1, 1)
    wait_in(1)
    attend(1)
    ring_turn(1, 2)
    ring_turn(1, 3)
    relay_out(1)
    wait_in(2)
    attend(2)
    ring_turn(2, 0)
    ring_turn(2, 1)
    relay_out(2)
    slab_wait(0, None)
    for h in range(3):
        wait_out(h)
    project(z)
    ring_turn(2, 2)
    slab_wait(0, 0)
    slab_wait(1, 0)
    project_pair(0)
    ring_turn(2, 3)
    slab_wait(0, 1)
    slab_wait(1, 1)
    project_pair(1)
    slab_wait(0, 2)
    slab_wait(1, 2)
    project_pair(2)
    for j in range(4):
        ring_turn(3, j)
    slab_wait(0, 3)
    project((z + 4) % 8)

    wait_bytes(ob.at[:, pl.ds(0, 2)], osem.at[4])
    wait_bytes(ob.at[:, pl.ds(0, 2)], osem.at[3])
    wait_bytes(ob.at[:, pl.ds(0, 2)], osem.at[0])
    wait_bytes(wx, osem.at[1])
    for h in range(3):
        wait_bytes(inb.at[h, pl.ds(0, 7)], in_send.at[h])
        wait_bytes(stage.at[h, pl.ds(0, 3), 0], out_send.at[h, 0])
        for i in (1, 2):
            wait_bytes(A.at[2, :, lanes_of(h, 0)], out_send.at[h, i])
        for i in range(4):
            wait_bytes(A.at[0, :, lanes_of(h, 0)], fsend.at[h, i])
    for part, sem in sent:
        wait_bytes(part, wsend.at[sem])
    assert count[0] <= wsend.shape[0] and len(sent) == count[0]


def body(queries, keys, values, query_tangent, key_tangent, value_tangent, out_weight):
    any_space = pl.BlockSpec(memory_space=pl.ANY)
    shape = jax.ShapeDtypeStruct((1, 128, 6144), BF16)
    return pl.pallas_call(
        kernel,
        name="attend_project",
        out_shape=(shape, shape),
        in_specs=[any_space] * 6 + [pl.BlockSpec(memory_space=pltpu.VMEM)],
        out_specs=(any_space, any_space),
        scratch_shapes=[
            pltpu.VMEM((8, 3, 2, 4, 2, 64, 384), BF16),
            pltpu.VMEM((3, 8, 128, 768), BF16),
            pltpu.VMEM((3, 4, 2, 2, 128, 128), BF16),
            pltpu.VMEM((4, 128, 3072), BF16),
            pltpu.VMEM((8, 4, 128, 384), BF16),
            pltpu.VMEM((3, 64, 192), BF16),
            pltpu.SemaphoreType.DMA((3,)),
            pltpu.SemaphoreType.DMA((3,)),
            pltpu.SemaphoreType.DMA((3,)),
            pltpu.SemaphoreType.DMA((3, 3)),
            pltpu.SemaphoreType.DMA((3, 3)),
            pltpu.SemaphoreType.DMA((3, 4)),
            pltpu.SemaphoreType.DMA((3, 4)),
            pltpu.SemaphoreType.DMA((96,)),
            pltpu.SemaphoreType.DMA((96,)),
            pltpu.SemaphoreType.DMA((5,)),
        ],
        compiler_params=pltpu.CompilerParams(
            collective_id=0, has_side_effects=True, vmem_limit_bytes=56 * 2**20
        ),
        cost_estimate=pl.CostEstimate(
            flops=17 * 10**9, bytes_accessed=8 * 2**20, transcendentals=3 * 2**20
        ),
    )(queries, keys, values, query_tangent, key_tangent, value_tangent, out_weight.reshape(3, 2, 64, 192))


def solution(mesh):
    placed = (P("fsdp", "seq", None),) * 6 + (P("seq", "fsdp"),)
    return jax.shard_map(
        body,
        mesh=mesh,
        in_specs=placed,
        out_specs=(P("fsdp", "seq", None), P("fsdp", "seq", None)),
        check_vma=False,
    )
```

time: 491 us -> 144 us (0.29)
  waiting for transfers between devices: 333 us -> 0 us
  Pallas kernels: 0 us -> 137 us
  matrix products: 57.6 us -> 0 us
  local copies, waits for them, and re-layouts: 40.6 us -> 5.68 us
  starting transfers between devices: 26.9 us -> 0 us
  other arithmetic: 17.5 us -> 0 us
  between operations: 14.2 us -> 0.65 us
    reduce_scatter x1 -> x0, waiting for transfers between devices: 266 us -> none  [body(): lax.psum_scatter(jnp.concatenate([jnp.dot(out, rows_weight, preferred_ele...]
    pallas_call x0 -> x1, Pallas kernels: none -> 137 us  [body(): pl.pallas_call(kernel, name='attend_project', out_shape=(shape, shape), i...]
    all_to_all x6 -> x0, waiting for transfers between devices: 49 us -> none  [the longest x1 11.4 us: body(): lax.all_to_all(local[1], 'seq', split_axis=1, concat_axis=0, tiled=True)]
    dot_general x12 -> x0, matrix products: 48.3 us -> none  [the longest x1 12.2 us: body(): jnp.dot(out, rows_weight, preferred_element_type=jnp.float32)]
    all_to_all x6 -> x0, starting transfers between devices: 26.8 us -> none  [the longest x1 7.48 us: body(): lax.all_to_all(local[0], 'seq', split_axis=1, concat_axis=0, tiled=True)]
    all_gather x1 -> x0, waiting for transfers between devices: 17.6 us -> none  [body(): rows_weight = lax.all_gather(out_weight, 'fsdp', axis=1, tiled=True)]
    concatenate x1 -> x0, other arithmetic: 17.5 us -> none  [body(): jnp.concatenate([jnp.dot(out, rows_weight, preferred_element_type=jnp.flo...]
    while x44 -> x0, local copies, waits for them, and re-layouts: 15 us -> none  [the longest x8 11 us: body(): out, out_dot = lax.map(one_block, (query_blocks, query_dot_blocks))]
  transfers between devices with their start and end apart: 8 -> 0, of which waited for: 7 -> 0; matrix products, arithmetic and copies ran while one was open for 13% -> 0% of each run, Pallas kernels for 0% -> 0%
where the time goes in v2:
time: 144 us
  Pallas kernels  137 us (95%)
  local copies, waits for them, and re-layouts  5.68 us (4%)
    pallas_call x1, Pallas kernels, body(): pl.pallas_call(kernel, name='attend_project', out_shape=(shape, shape), i...  137 us
    unnamed x5, local copies, waits for them, and re-layouts  5.68 us

profile of v2, /device:TPU:1, one launch (start us, length us, event | category | flops | bytes accessed | tf_op | source)
XLA Modules:
  0.0 143.7 jit_solution(3327603674985172172)
XLA Ops:
  0.6 1.7 %copy.9 = bf16[384,192]{1,0:T(8,128)(2,1)} copy(bf16[384,192]{0,1:T(8,128)(2,1)} %param.13) | data formatting | bytes 294912 | tf_op args[6]
  2.4 137.4 %attend_project.1 = (bf16[1,128,6144]{2,1,0:T(8,128)(2,1)}, bf16[1,128,6144]{2,1,0:T(8,128)(2,1)}) custom-call(bf16[1,128,3072]{2,1,0:T(8,128)(2,1)} %q.1, bf16[1,128,3072]{2,1,0:T(8,128)(2,1)} %k.1, bf16[1,128,3072]{2,1,0:T(8,128)(2,1)} %v.1, bf16[1,128,3072]{2,1,0:T(8,128)(2,1)} %qd.1, bf16[1,128,3072]{2,1,0:T(8,128)(2,1)} %kd.1, ...), custom_call_target="tpu_custom_call" | custom-call | flops 16999999488 | bytes 8388608 | tf_op jit(solution)/shard_map/attend_project/pallas_call | solution.py:326
  139.8 0.0 copy-start
  139.8 2.8 %copy.12 = bf16[1,128,6144]{2,1,0:T(8,128)(2,1)} copy(bf16[1,128,6144]{2,1,0:T(8,128)(2,1)} %get-tuple-element.4) | data formatting | bytes 3145728
  142.6 0.0 copy-done
  142.6 1.1 copy.13
Async XLA Ops:
  139.8 2.8 %copy-start = (bf16[1,128,6144]{2,1,0:T(8,128)(2,1)S(1)}, bf16[1,128,6144]{2,1,0:T(8,128)(2,1)}, u32[]{:S(2)}) copy-start(bf16[1,128,6144]{2,1,0:T(8,128)(2,1)} %get-tuple-element.5) | copy-start | bytes 4718596

commit v3 on v2

--- a/solution.py
+++ b/solution.py
@@ -15,7 +15,7 @@
 TURNS = (0, 1, 3, 2)
 
 
-def kernel(q, k, v, qd, kd, vd, w, mixed, mixed_dot, W, inb, stage, A, ob, wx,
+def kernel(q, k, v, qd, kd, vd, w, mixed, mixed_dot, W, inb, stage, A, ob, wx, wo, wide,
            in_send, in_recv, in_loc, out_send, out_recv, fsend, frecv, wsend, wrecv, osem):
     f, s = lax.axis_index("fsdp"), lax.axis_index("seq")
     xlo, z, c = f // 16, (f // 2) % 8, f % 2
@@ -69,19 +69,24 @@
 
     arrays = (qd, q, k, kd, v, vd)
 
+    def send_in_to(h, t):
+        for i, ref in enumerate(arrays):
+            pltpu.make_async_remote_copy(
+                src_ref=ref.at[0, :, pl.ds(pl.multiple_of(t * 384 + h * HD, HD), HD)],
+                dst_ref=inb.at[h, s, :, pl.ds(i * HD, HD)],
+                send_sem=in_send.at[h], recv_sem=in_recv.at[h],
+                device_id=(f, t), device_id_type=MESH,
+            ).start()
+
+    def send_in_x(h):
+        send_in_to(h, 2 * y + 1 - xhi)
+
     def send_in(h):
         def to(j, carry):
-            t = (s + j) % 8
-            for i, ref in enumerate(arrays):
-                pltpu.make_async_remote_copy(
-                    src_ref=ref.at[0, :, pl.ds(pl.multiple_of(t * 384 + h * HD, HD), HD)],
-                    dst_ref=inb.at[h, s, :, pl.ds(i * HD, HD)],
-                    send_sem=in_send.at[h], recv_sem=in_recv.at[h],
-                    device_id=(f, t), device_id_type=MESH,
-                ).start()
+            send_in_to(h, (2 * y + j) % 8)
             return carry
 
-        lax.fori_loop(1, 8, to, 0)
+        lax.fori_loop(2, 8, to, 0)
         for i, ref in enumerate(arrays):
             pltpu.make_async_copy(
                 ref.at[0, :, pl.ds(pl.multiple_of(s * 384 + h * HD, HD), HD)],
@@ -171,21 +176,24 @@
         wait_bytes(A.at[1, :, lanes_of(h, 1 - xhi)], frecv.at[h, 3])
 
     def prepare_send():
+        pltpu.make_async_copy(w, wo, osem.at[5]).start()
         pltpu.make_async_remote_copy(
-            src_ref=w.at[:, peer], dst_ref=wx, send_sem=osem.at[1], recv_sem=osem.at[2],
+            src_ref=w, dst_ref=wx, send_sem=osem.at[1], recv_sem=osem.at[2],
             device_id=mate, device_id_type=MESH,
         ).start()
 
     def prepare():
-        wait_bytes(wx, osem.at[2])
         row = lax.broadcasted_iota(jnp.int32, (192, 384), 0)
         lane = lax.broadcasted_iota(jnp.int32, (192, 384), 1)
         put_own = (lane == row + 192 * c).astype(BF16)
         put_other = (lane == row + 192 * peer).astype(BF16)
-        own = w[:, c].reshape(192, 192)
-        both = jnp.dot(own, put_own, preferred_element_type=F32)
-        both += jnp.dot(wx[...].reshape(192, 192), put_other, preferred_element_type=F32)
-        W[z, :, xhi, y, c] = both.astype(BF16).reshape(3, 64, 384)
+        tn = (((0,), (0,)), ((), ()))
+        wait_bytes(wo, osem.at[5])
+        both = lax.dot_general(wo[...], put_own, tn, preferred_element_type=F32)
+        wait_bytes(wx, osem.at[2])
+        both += lax.dot_general(wx[...], put_other, tn, preferred_element_type=F32)
+        wide[...] = both.astype(BF16).reshape(3, 2, 64, 384)
+        W[z, :, xhi, y, c] = wide[:, c]
 
     def chunk(slab, turn, core=None):
         return W.at[slab, :, :, (y + turn) % 4, c if core is None else core]
@@ -257,10 +265,13 @@
     prepare_send()
     prepare()
     plane_x()
+    send_in_x(0)
+    send_in_x(1)
     plane_y()
     ring_start(0)
     send_in(0)
     send_in(1)
+    send_in_x(2)
     send_in(2)
     ring_start(1)
     ring_start(2)
@@ -272,15 +283,15 @@
     ring_turn(0, 2)
     ring_turn(0, 3)
     ring_turn(1, 0)
-    relay_out(0)
     ring_turn(1, 1)
     wait_in(1)
     attend(1)
+    relay_out(0)
     ring_turn(1, 2)
     ring_turn(1, 3)
-    relay_out(1)
     wait_in(2)
     attend(2)
+    relay_out(1)
     ring_turn(2, 0)
     ring_turn(2, 1)
     relay_out(2)
@@ -327,7 +338,7 @@
         kernel,
         name="attend_project",
         out_shape=(shape, shape),
-        in_specs=[any_space] * 6 + [pl.BlockSpec(memory_space=pltpu.VMEM)],
+        in_specs=[any_space] * 7,
         out_specs=(any_space, any_space),
         scratch_shapes=[
             pltpu.VMEM((8, 3, 2, 4, 2, 64, 384), BF16),
@@ -335,7 +346,9 @@
             pltpu.VMEM((3, 4, 2, 2, 128, 128), BF16),
             pltpu.VMEM((4, 128, 3072), BF16),
             pltpu.VMEM((8, 4, 128, 384), BF16),
-            pltpu.VMEM((3, 64, 192), BF16),
+            pltpu.VMEM((192, 384), BF16),
+            pltpu.VMEM((192, 384), BF16),
+            pltpu.VMEM((3, 2, 64, 384), BF16),
             pltpu.SemaphoreType.DMA((3,)),
             pltpu.SemaphoreType.DMA((3,)),
             pltpu.SemaphoreType.DMA((3,)),
@@ -345,7 +358,7 @@
             pltpu.SemaphoreType.DMA((3, 4)),
             pltpu.SemaphoreType.DMA((96,)),
             pltpu.SemaphoreType.DMA((96,)),
-            pltpu.SemaphoreType.DMA((5,)),
+            pltpu.SemaphoreType.DMA((6,)),
         ],
         compiler_params=pltpu.CompilerParams(
             collective_id=0, has_side_effects=True, vmem_limit_bytes=56 * 2**20
@@ -353,7 +366,7 @@
         cost_estimate=pl.CostEstimate(
             flops=17 * 10**9, bytes_accessed=8 * 2**20, transcendentals=3 * 2**20
         ),
-    )(queries, keys, values, query_tangent, key_tangent, value_tangent, out_weight.reshape(3, 2, 64, 192))
+    )(queries, keys, values, query_tangent, key_tangent, value_tangent, out_weight.T)
 
 
 def solution(mesh):

time: 144 us -> 142 us (0.986)
  local copies, waits for them, and re-layouts: 5.68 us -> 3.95 us
    unnamed x5 -> x4, local copies, waits for them, and re-layouts: 5.68 us -> 3.95 us
where the time goes in v3:
time: 142 us
  Pallas kernels  137 us (96%)
  local copies, waits for them, and re-layouts  3.95 us (3%)
    pallas_call x1, Pallas kernels, body(): pl.pallas_call(kernel, name='attend_project', out_shape=(shape, shape), i...  137 us
    unnamed x4, local copies, waits for them, and re-layouts  3.95 us

profile of v3, /device:TPU:1, one launch (start us, length us, event | category | flops | bytes accessed | tf_op | source)
XLA Modules:
  0.0 141.7 jit_solution(14908589278740980635)
XLA Ops:
  0.6 137.1 %attend_project.1 = (bf16[1,128,6144]{2,1,0:T(8,128)(2,1)}, bf16[1,128,6144]{2,1,0:T(8,128)(2,1)}) custom-call(bf16[1,128,3072]{2,1,0:T(8,128)(2,1)} %q.1, bf16[1,128,3072]{2,1,0:T(8,128)(2,1)} %k.1, bf16[1,128,3072]{2,1,0:T(8,128)(2,1)} %v.1, bf16[1,128,3072]{2,1,0:T(8,128)(2,1)} %qd.1, bf16[1,128,3072]{2,1,0:T(8,128)(2,1)} %kd.1, ...), custom_call_target="tpu_custom_call" | custom-call | flops 16999999488 | bytes 8388608 | tf_op jit(solution)/shard_map/attend_project/pallas_call | solution.py:337
  137.7 0.0 copy-start
  137.7 2.8 %copy.11 = bf16[1,128,6144]{2,1,0:T(8,128)(2,1)} copy(bf16[1,128,6144]{2,1,0:T(8,128)(2,1)} %get-tuple-element.4) | data formatting | bytes 3145728
  140.5 0.0 copy-done
  140.5 1.1 copy.12
Async XLA Ops:
  137.7 2.8 %copy-start = (bf16[1,128,6144]{2,1,0:T(8,128)(2,1)S(1)}, bf16[1,128,6144]{2,1,0:T(8,128)(2,1)}, u32[]{:S(2)}) copy-start(bf16[1,128,6144]{2,1,0:T(8,128)(2,1)} %get-tuple-element.5) | copy-start | bytes 4718596

commit v4 on v3

--- a/solution.py
+++ b/solution.py
@@ -207,8 +207,11 @@
 
     def plane_y():
         landed(W.at[z, :, 1 - xhi, y, c], plane["x"])
-        for turn in (1, 3, 2):
+        for turn in (1, 3):
             plane[turn] = push(chunk(z, 0), dev(dy=4 - turn))
+
+    def plane_y_far():
+        plane[2] = push(chunk(z, 0), dev(dy=2))
 
     def ring_start(j):
         turn = TURNS[j]
@@ -270,6 +273,7 @@
     plane_y()
     ring_start(0)
     send_in(0)
+    plane_y_far()
     send_in(1)
     send_in_x(2)
     send_in(2)

time: 142 us -> 150 us (1.056)
  Pallas kernels: 137 us -> 145 us
    pallas_call x1, Pallas kernels: 137 us -> 145 us  [body(): pl.pallas_call(kernel, name='attend_project', out_shape=(shape, shape), i...]
where the time goes in v4:
time: 150 us
  Pallas kernels  145 us (97%)
  local copies, waits for them, and re-layouts  3.95 us (3%)
    pallas_call x1, Pallas kernels, body(): pl.pallas_call(kernel, name='attend_project', out_shape=(shape, shape), i...  145 us
    unnamed x4, local copies, waits for them, and re-layouts  3.95 us

profile of v4, /device:TPU:1, one launch (start us, length us, event | category | flops | bytes accessed | tf_op | source)
XLA Modules:
  0.0 150.0 jit_solution(14941446148928423788)
XLA Ops:
  0.6 145.4 %attend_project.1 = (bf16[1,128,6144]{2,1,0:T(8,128)(2,1)}, bf16[1,128,6144]{2,1,0:T(8,128)(2,1)}) custom-call(bf16[1,128,3072]{2,1,0:T(8,128)(2,1)} %q.1, bf16[1,128,3072]{2,1,0:T(8,128)(2,1)} %k.1, bf16[1,128,3072]{2,1,0:T(8,128)(2,1)} %v.1, bf16[1,128,3072]{2,1,0:T(8,128)(2,1)} %qd.1, bf16[1,128,3072]{2,1,0:T(8,128)(2,1)} %kd.1, ...), custom_call_target="tpu_custom_call" | custom-call | flops 16999999488 | bytes 8388608 | tf_op jit(solution)/shard_map/attend_project/pallas_call | solution.py:341
  146.0 0.0 copy-start
  146.0 2.8 %copy.11 = bf16[1,128,6144]{2,1,0:T(8,128)(2,1)} copy(bf16[1,128,6144]{2,1,0:T(8,128)(2,1)} %get-tuple-element.4) | data formatting | bytes 3145728
  148.8 0.0 copy-done
  148.8 1.1 copy.12
Async XLA Ops:
  146.0 2.8 %copy-start = (bf16[1,128,6144]{2,1,0:T(8,128)(2,1)S(1)}, bf16[1,128,6144]{2,1,0:T(8,128)(2,1)}, u32[]{:S(2)}) copy-start(bf16[1,128,6144]{2,1,0:T(8,128)(2,1)} %get-tuple-element.5) | copy-start | bytes 4718596
